TPU v7x, 512 devices: a whole 4x8x8 slice. The times are simulated.
512 devices in a mesh: ctx: 16 (over z_lo, x), tp: 16 (over z_hi, y), dp: 2 (over core).
Axes of the slice: x: 4, y: 8, z: 8 (z_hi: 2, z_lo: 4; z = z_hi * 4 + z_lo), core: 2. Of those that a mesh axis runs over, the one named last changes fastest.
Arguments:
- image_tokens: bfloat16 [16384, 3072], P(('dp', 'ctx', 'tp')), parts along dimension 0, may hold values from -50 to 50
- text_tokens: bfloat16 [512, 3072], P(('dp', 'tp')), parts along dimension 0, may hold values from -50 to 50
- image_modulation: float32 [6, 3072], P('dp'), parts along dimension 0, may hold values from -4 to 4
- text_modulation: float32 [6, 3072], P('dp'), parts along dimension 0, may hold values from -4 to 4
- image_projection: bfloat16 [3072, 6144], P(None, 'tp'), may hold values from -0.109375 to 0.109375
- text_projection: bfloat16 [3072, 6144], P('ctx', 'tp'), may hold values from -0.109375 to 0.109375
- image_merge: bfloat16 [2048, 3072], P('tp'), may hold values from -0.59765625 to 0.59765625
- text_merge: bfloat16 [2048, 3072], P('tp', 'ctx'), may hold values from -0.59765625 to 0.59765625
- norm_gains: float32 [4, 128], replicated, may hold values from 0.5 to 16
Outputs:
- image_update: bfloat16 [16384, 3072], P(('dp', 'ctx', 'tp')), parts along dimension 0
- text_update: bfloat16 [512, 3072], P(('dp', 'tp'), 'ctx'), parts along dimension 0
There are 2 independent parts, one for each index of `dp`. A program takes and returns all parts, laid end to end along the dimension named above; an argument that names none is the same for every part. Nothing has to cross between parts.
All inputs are finite; a program needn't handle non-finite values.
Results may differ from a plain program's by a relative error of at most 0.025.
The roundings to bfloat16 on the way count: a program that leaves them out, or rounds other values in their place, can miss the bound.
Values may be sent and summed in bfloat16 or wider, within the bound.
A program may use at most 64 MiB of HBM per device.

v0:
```python
import jax
import jax.numpy as jnp
from jax import lax
from jax.sharding import PartitionSpec as P

HEAD_DIM = 128


norm_epsilon = 1e-06
block_keys = 512


def layer_norm(tokens, modulation):
    tokens = tokens.astype(jnp.float32)
    centred = tokens - jnp.mean(tokens, axis=1, keepdims=True)
    scaled = centred * lax.rsqrt(jnp.mean(centred * centred, axis=1, keepdims=True) + norm_epsilon)
    return (scaled * (1.0 + modulation[1]) + modulation[0]).astype(jnp.bfloat16)


def head_norm(features, gain):
    normed = features * lax.rsqrt(
        jnp.mean(features * features, axis=-1, keepdims=True) + norm_epsilon
    )
    return (normed * gain).astype(jnp.bfloat16)


def head_parts(projected, gain_query, gain_key):
    heads_here = projected.shape[1] // (3 * HEAD_DIM)
    split = projected.reshape(projected.shape[0], heads_here, 3, HEAD_DIM)
    query = head_norm(split[:, :, 0], gain_query)
    keys = head_norm(split[:, :, 1], gain_key)
    values = split[:, :, 2].astype(jnp.bfloat16)
    return (query, keys, values)


def attend_block(carry, query_all, key_block, value_block):
    best, total, weighted = carry
    scores = jnp.einsum(
        "qhd,khd->hqk", query_all, key_block, preferred_element_type=jnp.float32
    ) * HEAD_DIM ** (-0.5)
    fresh = jnp.maximum(best, jnp.max(scores, axis=2))
    decay = jnp.exp(best - fresh)
    weights = jnp.exp(scores - fresh[:, :, None])
    total = total * decay + jnp.sum(weights, axis=2)
    weighted = weighted * decay[:, :, None] + jnp.einsum(
        "hqk,khd->hqd",
        weights.astype(jnp.bfloat16),
        value_block,
        preferred_element_type=jnp.float32,
    )
    return (fresh, total, weighted)


def on_device(
    image_tokens,
    text_tokens,
    image_modulation,
    text_modulation,
    image_projection,
    text_projection,
    image_merge,
    text_merge,
    norm_gains,
):
    image_in = layer_norm(image_tokens, image_modulation)
    text_in = layer_norm(text_tokens, text_modulation)
    image_proj = jnp.dot(
        lax.all_gather(image_in, "tp", axis=0, tiled=True),
        image_projection,
        preferred_element_type=jnp.float32,
    )
    text_full = lax.all_gather(text_in, "tp", axis=0, tiled=True)
    weight_full = lax.all_gather(text_projection, "ctx", axis=0, tiled=True)
    text_proj = jnp.dot(text_full, weight_full, preferred_element_type=jnp.float32)
    query_image, keys_image, values_image = head_parts(image_proj, norm_gains[0], norm_gains[1])
    query_text, keys_text, values_text = head_parts(text_proj, norm_gains[2], norm_gains[3])
    query_all = jnp.concatenate([query_image, query_text], axis=0)
    image_rows = query_image.shape[0]
    query_count = query_all.shape[0]
    heads_here = query_all.shape[1]

    def fold_keys(carry, piece):
        keys_in, values_in = piece
        count = keys_in.shape[0]
        width = block_keys if count % block_keys == 0 else count
        key_blocks = keys_in.reshape(count // width, width, heads_here, HEAD_DIM)
        value_blocks = values_in.reshape(count // width, width, heads_here, HEAD_DIM)

        def one_block(inner, blocks):
            return (attend_block(inner, query_all, blocks[0], blocks[1]), None)

        carry, unused = lax.scan(one_block, carry, (key_blocks, value_blocks))
        return carry

    start_carry = (
        jnp.full((heads_here, query_count), -1e30, jnp.float32),
        jnp.zeros((heads_here, query_count), jnp.float32),
        jnp.zeros((heads_here, query_count, HEAD_DIM), jnp.float32),
    )
    flat_width = heads_here * HEAD_DIM
    text_carry = fold_keys(
        start_carry, (keys_text.reshape(-1, flat_width), values_text.reshape(-1, flat_width))
    )
    best, total, weighted = fold_keys(
        text_carry,
        (
            lax.all_gather(keys_image.reshape(image_rows, flat_width), "ctx", axis=0, tiled=True),
            lax.all_gather(values_image.reshape(image_rows, flat_width), "ctx", axis=0, tiled=True),
        ),
    )
    attended = (weighted / total[:, :, None]).astype(jnp.bfloat16)
    attended = attended.transpose(1, 0, 2).reshape(query_count, flat_width)
    attn_image = attended[:image_rows]
    attn_text = attended[image_rows:]
    block = attn_image
    image_sum = lax.psum_scatter(
        jnp.dot(block, image_merge, preferred_element_type=jnp.float32).astype(jnp.bfloat16),
        "tp",
        scatter_dimension=0,
        tiled=True,
    ).astype(jnp.float32)
    image_update = (image_modulation[2] * image_sum).astype(jnp.bfloat16)
    block = attn_text
    text_sum = lax.psum_scatter(
        jnp.dot(block, text_merge, preferred_element_type=jnp.float32).astype(jnp.bfloat16),
        "tp",
        scatter_dimension=0,
        tiled=True,
    ).astype(jnp.float32)
    out_width = text_merge.shape[1]
    gate_columns = lax.dynamic_slice_in_dim(
        text_modulation[2], lax.axis_index("ctx") * out_width, out_width, 0
    )
    text_update = (gate_columns * text_sum).astype(jnp.bfloat16)
    return (image_update, text_update)


def solution(mesh):
    placed = (
        P(("dp", "ctx", "tp"), None),
        P(("dp", "tp"), None),
        P("dp", None),
        P("dp", None),
        P(None, "tp"),
        P("ctx", "tp"),
        P("tp", None),
        P("tp", "ctx"),
        P(),
    )
    return jax.shard_map(
        on_device,
        mesh=mesh,
        in_specs=placed,
        out_specs=(P(("dp", "ctx", "tp"), None), P(("dp", "tp"), "ctx")),
        check_vma=False,
    )
```

profile of v0, /device:TPU:2, one launch (start us, length us, event | category | flops | bytes accessed | tf_op | source)
XLA Modules:
  0.0 1001.3 jit_solution(11085889003317836134)
XLA Ops:
  10.6 1.7 fusion.21
  15.5 1.6 fusion.34
  17.9 119.3 %all-gather.7.cloned.1.call-done = bf16[512,3072]{1,0:T(8,128)(2,1)} async-done(((bf16[32,3072]{1,0:T(8,128)(2,1)}), bf16[512,3072]{1,0:T(8,128)(2,1)}) %all-gather.7.cloned.1.call-update) | async-done | bytes 3145744 | tf_op jit(solution)/shard_map/all_gather | solution.py:68
  137.3 3.3 fusion.47
  144.6 89.7 %all-gather.9.cloned.1.call-done = bf16[256,3072]{1,0:T(8,128)(2,1)} async-done(((bf16[16,3072]{1,0:T(8,128)(2,1)}), bf16[256,3072]{1,0:T(8,128)(2,1)}) %all-gather.9.cloned.1.call-update) | async-done | bytes 1572880 | tf_op jit(solution)/shard_map/all_gather | solution.py:72
  234.3 81.9 %all-gather.11.cloned.1.call-done = bf16[3072,384]{1,0:T(8,128)(2,1)} async-done(((bf16[192,384]{1,0:T(8,128)(2,1)}), bf16[3072,384]{1,0:T(8,128)(2,1)}) %all-gather.11.cloned.1.call-update) | async-done | bytes 2359312 | tf_op jit(solution)/shard_map/all_gather | solution.py:73
  316.2 3.2 fusion.48
  321.1 81.7 %all-gather.15.cloned.1.call-done = bf16[8192,1,1,128]{3,0,2,1:T(8,128)(2,1)} async-done(((bf16[512,1,1,128]{3,0,2,1:T(8,128)(2,1)}), bf16[8192,1,1,128]{3,0,2,1:T(8,128)(2,1)}) %all-gather.15.cloned.1.call-update) | async-done | bytes 2097168 | tf_op jit(solution)/shard_map/all_gather | solution.py:108
  402.8 87.0 %all-gather.13.cloned.1.call-done = bf16[8192,128]{1,0:T(8,128)(2,1)} async-done(((bf16[512,128]{1,0:T(8,128)(2,1)}), bf16[8192,128]{1,0:T(8,128)(2,1)}) %all-gather.13.cloned.1.call-update) | async-done | bytes 2097168 | tf_op jit(solution)/shard_map/all_gather | solution.py:107
  489.8 49.2 %while.2 = (s32[]{:T(128)}, f32[1,768]{1,0:T(1,128)S(1)}, f32[1,768]{1,0:T(1,128)S(1)}, f32[1,768,128]{2,1,0:T(8,128)S(1)}, bf16[16,512,1,128]{3,1,2,0:T(8,128)(...) while((s32[]{:T(128)}, f32[1,768]{1,0:T(1,128)S(1)}, ...), condition=%wide.region_13.14_spmd, body=%wide.region_10.13_spmd.sunk | while | flops 203884800 | bytes 6016101 | solution.py:92
  489.8 1.3 fusion.63
  491.4 1.4 fusion.66
  494.4 1.4 fusion.66
  497.5 1.4 fusion.66
  500.6 1.4 fusion.66
  503.7 1.4 fusion.66
  506.7 1.4 fusion.66
  509.8 1.4 fusion.66
  512.9 1.4 fusion.66
  516.0 1.4 fusion.66
  519.0 1.4 fusion.66
  522.1 1.4 fusion.66
  525.2 1.4 fusion.66
  528.2 1.4 fusion.66
  531.3 1.4 fusion.66
  534.4 1.4 fusion.66
  537.5 1.4 fusion.66
  540.1 3.8 convolution_convert_fusion
  544.0 212.4 %reduce-scatter.5.cloned.1.call-done = bf16[16,192]{1,0:T(8,128)(2,1)} async-done(((bf16[256,192]{1,0:T(8,128)(2,1)}), bf16[16,192]{1,0:T(8,128)(2,1)}) %reduce-scatter.5.cloned.1.call-update) | async-done | bytes 6160 | tf_op jit(solution)/shard_map/reduce_scatter | solution.py:124
  756.4 1.3 multiply_convert_fusion.3
  757.7 235.2 %reduce-scatter.3.cloned.1.call-done = bf16[32,3072]{1,0:T(8,128)(2,1)} async-done(((bf16[512,3072]{1,0:T(8,128)(2,1)}), bf16[32,3072]{1,0:T(8,128)(2,1)}) %reduce-scatter.3.cloned.1.call-update) | async-done | bytes 196624 | tf_op jit(solution)/shard_map/reduce_scatter | solution.py:116
  992.9 1.6 multiply_convert_fusion
  (140 shorter events, 38.1 us)
Async XLA Ops:
  7.2 130.1 %copy-start = (bf16[3072,384]{1,0:T(8,128)(2,1)S(1)}, bf16[3072,384]{1,0:T(8,128)(2,1)}, u32[]{:S(2)}) copy-start(bf16[3072,384]{1,0:T(8,128)(2,1)} %param.15) | copy-start | bytes 7077892
  7.2 130.1 %all-gather.7.cloned.1.call-start = ((), (), s32[]{:S(2)}) async-start(), calls=%async_computation.2 | async-start | bytes 3342336 | tf_op jit(solution)/shard_map/all_gather | solution.py:68
  12.3 221.9 %all-gather.9.cloned.1.call-start = ((), (), s32[]{:S(2)}) async-start(), calls=%async_computation.3 | async-start | bytes 1671168 | tf_op jit(solution)/shard_map/all_gather | solution.py:72
  17.2 299.1 %all-gather.11.cloned.1.call-start = ((), (), s32[]{:S(2)}) async-start(), calls=%async_computation.4 | async-start | bytes 2506752 | tf_op jit(solution)/shard_map/all_gather | solution.py:73
  17.9 124.5 %copy-start.3 = (f32[4,128]{1,0:T(4,128)S(1)}, f32[4,128]{1,0:T(4,128)}, u32[]{:S(2)}) copy-start(f32[4,128]{1,0:T(4,128)} %param.19) | copy-start | bytes 6148
  17.9 384.9 %all-gather.15.cloned.1.call-start = ((), (), s32[]{:S(2)}) async-start(), calls=%async_computation.8 | async-start | bytes 2228224 | tf_op jit(solution)/shard_map/all_gather | solution.py:108
  140.6 0.9 copy-start.1
  142.3 347.5 %all-gather.13.cloned.1.call-start = ((), (), s32[]{:S(2)}) async-start(), calls=%async_computation.5 | async-start | bytes 2228224 | tf_op jit(solution)/shard_map/all_gather | solution.py:107
  144.6 611.8 %reduce-scatter.5.cloned.1.call-start = ((), (), s32[]{:S(2)}) async-start(), calls=%async_computation.7 | async-start | bytes 139264 | tf_op jit(solution)/shard_map/reduce_scatter | solution.py:124
  489.8 49.4 %copy-start.2 = (bf16[128,192]{0,1:T(8,128)(2,1)S(1)}, bf16[128,192]{0,1:T(8,128)(2,1)}, u32[]{:S(2)}) copy-start(bf16[128,192]{0,1:T(8,128)(2,1)} %param.18) | copy-start | bytes 147460
  540.1 452.8 %reduce-scatter.3.cloned.1.call-start = ((), (), s32[]{:S(2)}) async-start(), calls=%async_computation.6 | async-start | bytes 3342336 | tf_op jit(solution)/shard_map/reduce_scatter | solution.py:116
Sparse Core Ops, SparseCore 0:
  12.5 124.7 all-gather.6
  140.5 93.7 all-gather.8
  236.4 79.8 all-gather.10
  318.2 84.5 all-gather.14
  405.3 84.4 all-gather.12
  540.2 216.1 reduce-scatter.4
  761.7 231.1 reduce-scatter.2
where the time goes:
time: 1000 us
  waiting for transfers between devices  908 us (91%)
  matrix products  55.4 us (6%)
  other arithmetic  19.3 us (2%)
  between operations  14.4 us (1%)
    reduce_scatter x1, waiting for transfers between devices, on_device(): lax.psum_scatter(jnp.dot(block, image_merge, preferred_element_type=jnp.f...  235 us
    reduce_scatter x1, waiting for transfers between devices, on_device(): lax.psum_scatter(jnp.dot(block, text_merge, preferred_element_type=jnp.fl...  212 us
    all_gather x1, waiting for transfers between devices, on_device(): lax.all_gather(image_in, 'tp', axis=0, tiled=True)  119 us
    all_gather x1, waiting for transfers between devices, on_device(): text_full = lax.all_gather(text_in, 'tp', axis=0, tiled=True)  89.7 us
    all_gather x1, waiting for transfers between devices, on_device(): lax.all_gather(keys_image.reshape(image_rows, flat_width), 'ctx', axis=0,...  87 us
    all_gather x1, waiting for transfers between devices, on_device(): weight_full = lax.all_gather(text_projection, 'ctx', axis=0, tiled=True)  81.9 us
    all_gather x1, waiting for transfers between devices, on_device(): lax.all_gather(values_image.reshape(image_rows, flat_width), 'ctx', axis=...  81.7 us
    dot_general x17, matrix products, attend_block(): jnp.einsum('hqk,khd->hqd', weights.astype(jnp.bfloat16), value_block, pre...  23.4 us
  transfers between devices with their start and end apart: 7, of which 7 were waited for; matrix products, arithmetic and copies ran while one was open for 2% of the time, Pallas kernels for 0%

commit v1 on v0

v1 whole, which is shorter than its diff:
```python
import jax
import jax.numpy as jnp
from jax import lax
from jax.experimental import pallas as pl
from jax.experimental.pallas import tpu as pltpu
from jax.sharding import PartitionSpec as P

HEAD_DIM = 128
D = 3072
EPS = 1e-06
NX, NZ, NY, NCTX, NTP = 4, 4, 8, 16, 16
ROWS = 32
TROWS = 16
CHUNKS = ((0,), (1, 7), (2, 6), (3, 5), (4,))
START = (0, 64, 192, 320, 448)
COUNT = (64, 128, 128, 128, 64)
NQ = 512 + TROWS
F32, BF16 = jnp.float32, jnp.bfloat16
LOG2E = 1.4426950408889634


def offset(r, h):
    for c, members in enumerate(CHUNKS):
        if r in members:
            return START[c] + (h * len(members) + members.index(r)) * ROWS


def layer_norm(tokens, modulation):
    tokens = tokens.astype(F32)
    centred = tokens - jnp.mean(tokens, axis=1, keepdims=True)
    scaled = centred * lax.rsqrt(jnp.mean(centred * centred, axis=1, keepdims=True) + EPS)
    return (scaled * (1.0 + modulation[1:2]) + modulation[0:1]).astype(BF16)


def head_norm(features, gain):
    normed = features * lax.rsqrt(jnp.mean(features * features, axis=1, keepdims=True) + EPS)
    return (normed * gain).astype(BF16)


def arrived(ref, sem):
    pltpu.make_async_copy(ref, ref, sem).wait()


def kernel(
    img, txt, imod, tmod, wp_in, wt, wm_in, wtm, gains,
    out_i, out_t,
    g, wp, w2, kv, kvt, q, tf, tsl, tpart, trcv, o, ox, to, top, tor, rr, rl, sr, sl,
    local_sem, a_send, a_recv, z_send, z_recv, x_send, x_recv,
    ts_send, ts_recv, tp_send, tp_recv, tk_send, tk_recv, to_send, to_recv, tm_send, tm_recv,
    w_send, w_recv, o_send, o_recv, r_send, r_recv,
):
    ctx, tp, dp = lax.axis_index("ctx"), lax.axis_index("tp"), lax.axis_index("dp")
    x, z = lax.rem(ctx, NX), lax.div(ctx, NX)
    y, hi = lax.rem(tp, NY), lax.div(tp, NY)
    mirror = {"ctx": (NZ - 1 - z) * NX + x, "tp": lax.rem(tp + NY, NTP)}
    y_left = {"tp": hi * NY + lax.rem(y + NY - 1, NY)}
    y_right = {"tp": hi * NY + lax.rem(y + 1, NY)}
    x_left = {"ctx": z * NX + lax.rem(x + NX - 1, NX)}
    x_right = {"ctx": z * NX + lax.rem(x + 1, NX)}
    other_core = {"dp": 1 - dp}
    pending = []

    def send(src, dst, ss, rs, device, when=None):
        def go():
            pltpu.make_async_remote_copy(
                src_ref=src, dst_ref=dst, send_sem=ss, recv_sem=rs,
                device_id=device, device_id_type=pl.DeviceIdType.MESH,
            ).start()

        if when is None:
            go()
        else:
            pl.when(when)(go)
        pending.append((src, ss, when))

    def peers(axis, own, count, act):
        def step(i, carry):
            act(lax.rem(own + i, count))
            return carry

        lax.fori_loop(1, count, step, 0)

    barrier = pltpu.get_barrier_semaphore()

    def greet(device):
        pl.semaphore_signal(barrier, inc=1, device_id=device, device_id_type=pl.DeviceIdType.MESH)

    peers("tp", tp, NTP, lambda i: greet({"tp": i}))
    peers("ctx", ctx, NCTX, lambda i: greet({"ctx": i}))
    greet(mirror)
    greet(other_core)

    load_wp = pltpu.make_async_copy(wp_in, wp, local_sem.at[0])
    load_wp.start()
    load_wm = pltpu.make_async_copy(wm_in, w2.at[pl.ds(0, HEAD_DIM)], local_sem.at[1])
    load_wm.start()

    g[0:ROWS, :] = layer_norm(img[...], imod[...])
    tf[...] = layer_norm(txt[...], tmod[...]).astype(F32)

    def columns_of(ref, rows, who):
        base = pl.multiple_of(lax.div(who * 3, 2) * 128, 128)
        wide = ref[rows, pl.ds(base, 256)]
        return jnp.where(lax.rem(who, 2) == 1, pltpu.roll(wide, 192, 1), wide)

    tsl[tp] = columns_of(tf, slice(0, TROWS), ctx).astype(BF16)

    pl.semaphore_wait(barrier, 2 * (NTP - 1) + 2)

    def rows_of(r, h, part=None):
        if part is None:
            return g.at[pl.ds(offset(r, h), ROWS)]
        return g.at[pl.ds(offset(r, h) + part * (ROWS // 2), ROWS // 2)]

    def forward(r, h, side):
        device = y_left if side == 0 else y_right
        there = r + 1 if side == 0 else (r + NY - 1) % NY
        hop = r if side == 0 else (NY - r) % NY
        if there == 4:
            send(rows_of(r, h, side), rows_of(4, h, side), a_send.at[side, hop, h], a_recv.at[4 + 4 * side, h], device)
        else:
            send(rows_of(r, h), rows_of(there, h), a_send.at[side, hop, h], a_recv.at[there, h], device)

    send(rows_of(0, 0), rows_of(0, 1), a_send.at[0, 4, 0], a_recv.at[0, 1], mirror)
    forward(0, 0, 0)
    forward(0, 0, 1)

    def send_text(i):
        pltpu.make_async_remote_copy(
            src_ref=tsl.at[tp], dst_ref=tsl.at[tp], send_sem=ts_send.at[i], recv_sem=ts_recv.at[tp],
            device_id={"tp": i}, device_id_type=pl.DeviceIdType.MESH,
        ).start()

    peers("tp", tp, NTP, send_text)

    piece = x * 2 + dp

    def merge_piece(p):
        return w2.at[pl.ds(pl.multiple_of(HEAD_DIM + p * 16, 16), 16)]

    load_wm.wait()
    send(w2.at[pl.ds(pl.multiple_of(piece * 16, 16), 16)], merge_piece(piece), w_send.at[0], w_recv.at[0], mirror)

    arrived(rows_of(0, 1), a_recv.at[0, 1])
    forward(0, 1, 0)
    forward(0, 1, 1)

    gain = [gains[i : i + 1, :] for i in range(4)]

    def project(c):
        rows = pl.ds(START[c], COUNT[c])
        out = jnp.dot(g[rows, :], wp[...], preferred_element_type=F32)
        q[rows, :] = head_norm(out[:, 0:128], gain[0])
        kv[z * NX, rows, 0:128] = head_norm(out[:, 128:256], gain[1])
        kv[z * NX, rows, 128:256] = out[:, 256:384].astype(BF16)

    def kv_rows(zs, rx, c, part=None):
        count = COUNT[c] if part is None else COUNT[c] // 2
        return kv.at[zs * NX + rx, pl.ds(START[c] + (0 if part is None else part * count), count)]

    def z_hop(c, zs, up):
        to_z = z + 1 if up else z - 1
        valid = (z < NZ - 1) if up else (z > 0)
        return to_z, valid

    def send_z(c, k, up):
        zs = z - k if up else z + k
        to_z = z + 1 if up else z - 1
        ok = (zs >= 0) & (to_z < NZ) if up else (zs < NZ) & (to_z >= 0)
        where = kv_rows(zs, 0, c)
        send(where, where, z_send.at[c, k, int(up)], z_recv.at[c, zs], {"ctx": to_z * NX + x}, ok)

    def source(k):
        return (z - k, z - k >= 0), (z + k, z + k < NZ)

    def send_x(c, zs, ok):
        mine = kv_rows(zs, 0, c)
        send(mine, kv_rows(zs, 1, c), x_send.at[c, zs, 0], x_recv.at[c, zs, 0], x_left, ok)
        send(mine, kv_rows(zs, 3, c), x_send.at[c, zs, 1], x_recv.at[c, zs, 1], x_right, ok)

    def pass_x(c, zs, ok):
        def wait(rx, i):
            arrived(kv_rows(zs, rx, c), x_recv.at[c, zs, i])

        if ok is None:
            wait(1, 0)
        else:
            pl.when(ok)(lambda: wait(1, 0))
        send(kv_rows(zs, 1, c, 0), kv_rows(zs, 2, c, 0), x_send.at[c, zs, 2], x_recv.at[c, zs, 2], x_left, ok)
        if ok is None:
            wait(3, 1)
        else:
            pl.when(ok)(lambda: wait(3, 1))
        send(kv_rows(zs, 3, c, 1), kv_rows(zs, 2, c, 1), x_send.at[c, zs, 3], x_recv.at[c, zs, 3], x_right, ok)

    def stage(c, n):
        if n == 0:
            send_z(c, 0, True)
            send_z(c, 0, False)
            send_x(c, z, None)
        elif n <= 3:
            for up, (zs, ok) in zip((True, False), source(n)):
                pl.when(ok)(lambda: arrived(kv_rows(zs, 0, c), z_recv.at[c, zs]))
                if n < 3:
                    send_z(c, n, up)
                send_x(c, zs, ok)
        elif n == 4:
            pass_x(c, z, None)
        else:
            for zs, ok in source(n - 4):
                pass_x(c, zs, ok)

    arrived(wp, local_sem.at[0])
    project(0)
    stage(0, 0)

    peers("tp", tp, NTP, lambda i: arrived(tsl.at[i], ts_recv.at[i]))
    text_part = jnp.dot(
        tsl[...].reshape(NTP * TROWS, 256)[:, 0:192], wt[...], preferred_element_type=F32
    )
    tpart[...] = text_part.reshape(NCTX, TROWS, 384)

    def send_part(i):
        pltpu.make_async_remote_copy(
            src_ref=tpart.at[i], dst_ref=trcv.at[ctx], send_sem=tp_send.at[i], recv_sem=tp_recv.at[ctx],
            device_id={"ctx": i}, device_id_type=pl.DeviceIdType.MESH,
        ).start()

    peers("ctx", ctx, NCTX, send_part)

    def merge_weights(step):
        if step == 0:
            arrived(merge_piece(piece), w_recv.at[0])
            for i in range(1, NX):
                send(
                    merge_piece(piece), merge_piece(piece), w_send.at[i], w_recv.at[i],
                    {"ctx": z * NX + lax.rem(x + i, NX)},
                )
        elif step == 1:
            for i in range(1, NX):
                theirs = lax.rem(x + NX - i, NX) * 2 + dp
                arrived(merge_piece(theirs), w_recv.at[i])
            for i in range(NX):
                p = i * 2 + dp
                send(merge_piece(p), merge_piece(p), w_send.at[4 + i], w_recv.at[4 + i], other_core)
        else:
            for i in range(NX):
                arrived(merge_piece(i * 2 + 1 - dp), w_recv.at[4 + i])

    def text_heads():
        peers("ctx", ctx, NCTX, lambda i: arrived(trcv.at[i], tp_recv.at[i]))
        trcv[ctx] = tpart[ctx]
        total = jnp.sum(trcv[...], axis=0)
        q[512:NQ, :] = head_norm(total[:, 0:128], gain[2])
        mine = pl.ds(pl.multiple_of(ctx * TROWS, TROWS), TROWS)
        kvt[mine, 0:128] = head_norm(total[:, 128:256], gain[3])
        kvt[mine, 128:256] = total[:, 256:384].astype(BF16)

        def send_keys(i):
            pltpu.make_async_remote_copy(
                src_ref=kvt.at[mine], dst_ref=kvt.at[mine], send_sem=tk_send.at[i], recv_sem=tk_recv.at[ctx],
                device_id={"ctx": i}, device_id_type=pl.DeviceIdType.MESH,
            ).start()

        peers("ctx", ctx, NCTX, send_keys)

    for d in (1, 2, 3):
        for h in (0, 1):
            arrived(rows_of(d, h), a_recv.at[d, h])
            forward(d, h, 0)
            arrived(rows_of(NY - d, h), a_recv.at[NY - d, h])
            forward(NY - d, h, 1)
            if h == 0:
                stage(d - 1, 1)
        project(d)
        stage(d, 0)
        for n in (2, 3, 4, 5, 6, 7):
            stage(d - 1, n)
        if d == 1:
            merge_weights(0)
            text_heads()
        if d == 2:
            merge_weights(1)
    for h in (0, 1):
        arrived(rows_of(4, h, 0), a_recv.at[4, h])
        arrived(rows_of(4, h, 1), a_recv.at[8, h])
    project(4)
    stage(4, 0)
    for n in (1, 2, 3, 4, 5, 6, 7):
        stage(3, n)
    for n in (1, 2, 3, 4, 5, 6, 7):
        stage(4, n)

    def last_x(c, zs, ok):
        def wait():
            arrived(kv_rows(zs, 2, c, 0), x_recv.at[c, zs, 2])
            arrived(kv_rows(zs, 2, c, 1), x_recv.at[c, zs, 3])

        if ok is None:
            wait()
        else:
            pl.when(ok)(wait)

    for c in range(5):
        last_x(c, z, None)
        for k in (1, 2, 3):
            for zs, ok in source(k):
                last_x(c, zs, ok)

    def text_rows(i):
        return kvt.at[pl.ds(pl.multiple_of(i * TROWS, TROWS), TROWS)]

    peers("ctx", ctx, NCTX, lambda i: arrived(text_rows(i), tk_recv.at[i]))
    merge_weights(2)

    scale = HEAD_DIM**-0.5 * LOG2E

    def attend(first, count):
        query = q[pl.ds(first, count), :]

        def block(carry, keys, values):
            best, total, weighted = carry
            s = lax.dot_general(query, keys, (((1,), (1,)), ((), ())), preferred_element_type=F32)
            fresh = jnp.maximum(best, jnp.max(s, axis=1, keepdims=True))
            decay = jnp.exp2((best - fresh) * scale)
            weights = jnp.exp2((s - fresh) * scale)
            total = total * decay + jnp.sum(weights, axis=1, keepdims=True)
            weighted = weighted * decay + jnp.dot(weights.astype(BF16), values, preferred_element_type=F32)
            return fresh, total, weighted

        carry = (
            jnp.full((count, 1), -1e30, F32),
            jnp.zeros((count, 1), F32),
            jnp.zeros((count, HEAD_DIM), F32),
        )
        carry = block(carry, kvt[:, 0:128], kvt[:, 128:256])

        def step(i, carry):
            both = kv[pl.ds(i * 2, 2)].reshape(1024, 256)
            return block(carry, both[:, 0:128], both[:, 128:256])

        best, total, weighted = lax.fori_loop(0, 8, step, carry)
        return (weighted / total).astype(BF16)

    def merge(c):
        rows = COUNT[c] // 2
        return jnp.dot(o[pl.ds(START[c] // 2, rows), :], w2[...], preferred_element_type=F32)

    def exchange(c):
        half = COUNT[c] // 2
        rows = pl.ds(START[c] // 2, half)
        count = COUNT[c] + (TROWS if c == 4 else 0)
        mixed = attend(START[c], count)
        o[rows, 0:128] = mixed[0:half]
        ox[rows, :] = mixed[half : 2 * half]
        send(ox.at[rows], o.at[rows, pl.ds(128, 128)], o_send.at[c], o_recv.at[c], mirror)
        if c == 4:
            to[ctx] = mixed[2 * half :]

            def send_out(i):
                pltpu.make_async_remote_copy(
                    src_ref=to.at[ctx], dst_ref=to.at[ctx], send_sem=to_send.at[i], recv_sem=to_recv.at[ctx],
                    device_id={"ctx": i}, device_id_type=pl.DeviceIdType.MESH,
                ).start()

            peers("ctx", ctx, NCTX, send_out)

    def text_merge():
        peers("ctx", ctx, NCTX, lambda i: arrived(to.at[i], to_recv.at[i]))
        part = jnp.dot(to[...].reshape(NCTX * TROWS, HEAD_DIM), wtm[...], preferred_element_type=F32)
        top[:, :, 0:192] = part.reshape(NTP, TROWS, 192)
        top[:, :, 192:256] = jnp.zeros((NTP, TROWS, 64), F32)

        def send_sum(i):
            pltpu.make_async_remote_copy(
                src_ref=top.at[i], dst_ref=tor.at[tp], send_sem=tm_send.at[i], recv_sem=tm_recv.at[tp],
                device_id={"tp": i}, device_id_type=pl.DeviceIdType.MESH,
            ).start()

        peers("tp", tp, NTP, send_sum)

    def reduce(c):
        rows = pl.ds(START[c] // 2, COUNT[c] // 2)
        arrived(o.at[rows, pl.ds(128, 128)], o_recv.at[c])
        part = merge(c)
        half = ROWS // 2
        if c == 4:
            sr[3, 0:half, :] = part[0:half].astype(BF16)
            sl[3, 0:half, :] = part[half:].astype(BF16)
            send(sr.at[3, pl.ds(0, half)], rr.at[3, pl.ds(0, half)], r_send.at[0, 3], r_recv.at[0, 3], y_right)
            send(sl.at[3, pl.ds(0, half)], rl.at[3, pl.ds(0, half)], r_send.at[1, 3], r_recv.at[1, 3], y_left)
            return
        if c == 0:
            arrived(rr.at[0], r_recv.at[0, 0])
            arrived(rl.at[0], r_recv.at[1, 0])
            total = part + rr[0].astype(F32) + rl[0].astype(F32)
            out_i[...] = (imod[2:3, :] * total).astype(BF16)
            return
        if c == 3:
            arrived(rr.at[3, pl.ds(0, half)], r_recv.at[0, 3])
            sr[2, 0:half, :] = (part[0:half] + rr[3, 0:half, :].astype(F32)).astype(BF16)
            sr[2, half:, :] = part[half:ROWS].astype(BF16)
        else:
            arrived(rr.at[c], r_recv.at[0, c])
            sr[c - 1] = (part[0:ROWS] + rr[c].astype(F32)).astype(BF16)
        send(sr.at[c - 1], rr.at[c - 1], r_send.at[0, c - 1], r_recv.at[0, c - 1], y_right)
        if c == 3:
            arrived(rl.at[3, pl.ds(0, half)], r_recv.at[1, 3])
            sl[2, 0:half, :] = part[ROWS : ROWS + half].astype(BF16)
            sl[2, half:, :] = (part[ROWS + half :] + rl[3, 0:half, :].astype(F32)).astype(BF16)
        else:
            arrived(rl.at[c], r_recv.at[1, c])
            sl[c - 1] = (part[ROWS:] + rl[c].astype(F32)).astype(BF16)
        send(sl.at[c - 1], rl.at[c - 1], r_send.at[1, c - 1], r_recv.at[1, c - 1], y_left)

    exchange(4)
    exchange(3)
    reduce(4)
    text_merge()
    exchange(2)
    reduce(3)
    exchange(1)
    reduce(2)
    exchange(0)
    reduce(1)

    peers("tp", tp, NTP, lambda i: arrived(tor.at[i], tm_recv.at[i]))
    tor[tp] = top[tp]
    text_total = jnp.sum(tor[...], axis=0)[:, 0:192]
    tf[0:3, :] = tmod[...]
    gate = columns_of(tf, slice(2, 3), ctx)[:, 0:192]
    out_t[...] = (gate * text_total).astype(BF16)

    reduce(0)

    for src, sem, when in pending:
        if when is None:
            arrived(src, sem)
        else:
            pl.when(when)(lambda: arrived(src, sem))
    peers("tp", tp, NTP, lambda i: arrived(tsl.at[tp], ts_send.at[i]))
    peers("ctx", ctx, NCTX, lambda i: arrived(tpart.at[i], tp_send.at[i]))
    peers("ctx", ctx, NCTX, lambda i: arrived(text_rows(ctx), tk_send.at[i]))
    peers("ctx", ctx, NCTX, lambda i: arrived(to.at[ctx], to_send.at[i]))
    peers("tp", tp, NTP, lambda i: arrived(top.at[i], tm_send.at[i]))


def on_device(*arrays):
    dma = pltpu.SemaphoreType.DMA
    vmem = pl.BlockSpec(memory_space=pltpu.VMEM)
    hbm = pl.BlockSpec(memory_space=pl.ANY)
    return pl.pallas_call(
        kernel,
        out_shape=(
            jax.ShapeDtypeStruct((ROWS, D), BF16),
            jax.ShapeDtypeStruct((TROWS, 192), BF16),
        ),
        in_specs=[vmem, vmem, vmem, vmem, hbm, vmem, hbm, vmem, vmem],
        out_specs=(vmem, vmem),
        scratch_shapes=[
            pltpu.VMEM((512, D), BF16),
            pltpu.VMEM((D, 384), BF16),
            pltpu.VMEM((256, D), BF16),
            pltpu.VMEM((NCTX, 512, 256), BF16),
            pltpu.VMEM((NCTX * TROWS, 256), BF16),
            pltpu.VMEM((NQ, HEAD_DIM), BF16),
            pltpu.VMEM((TROWS, D), F32),
            pltpu.VMEM((NTP, TROWS, 256), BF16),
            pltpu.VMEM((NCTX, TROWS, 384), F32),
            pltpu.VMEM((NCTX, TROWS, 384), F32),
            pltpu.VMEM((256, 256), BF16),
            pltpu.VMEM((256, HEAD_DIM), BF16),
            pltpu.VMEM((NCTX, TROWS, HEAD_DIM), BF16),
            pltpu.VMEM((NTP, TROWS, 256), F32),
            pltpu.VMEM((NTP, TROWS, 256), F32),
            pltpu.VMEM((4, ROWS, D), BF16),
            pltpu.VMEM((4, ROWS, D), BF16),
            pltpu.VMEM((4, ROWS, D), BF16),
            pltpu.VMEM((4, ROWS, D), BF16),
            dma((2,)),
            dma((2, 5, 2)),
            dma((9, 2)),
            dma((5, 3, 2)),
            dma((5, NZ)),
            dma((5, NZ, 4)),
            dma((5, NZ, 4)),
            dma((NTP,)), dma((NTP,)),
            dma((NCTX,)), dma((NCTX,)),
            dma((NCTX,)), dma((NCTX,)),
            dma((NCTX,)), dma((NCTX,)),
            dma((NTP,)), dma((NTP,)),
            dma((8,)), dma((8,)),
            dma((5,)), dma((5,)),
            dma((2, 4)), dma((2, 4)),
        ],
        compiler_params=pltpu.CompilerParams(
            collective_id=0, has_side_effects=True, vmem_limit_bytes=48 * 1024 * 1024
        ),
        cost_estimate=pl.CostEstimate(flops=7_000_000_000, bytes_accessed=8_000_000, transcendentals=4_500_000),
        name="joint_attention",
    )(*arrays)


def solution(mesh):
    placed = (
        P(("dp", "ctx", "tp"), None),
        P(("dp", "tp"), None),
        P("dp", None),
        P("dp", None),
        P(None, "tp"),
        P("ctx", "tp"),
        P("tp", None),
        P("tp", "ctx"),
        P(),
    )
    return jax.shard_map(
        on_device,
        mesh=mesh,
        in_specs=placed,
        out_specs=(P(("dp", "ctx", "tp"), None), P(("dp", "tp"), "ctx")),
        check_vma=False,
    )
```

time: 1000 us -> 135 us (0.14)
  waiting for transfers between devices: 908 us -> 0 us
  Pallas kernels: 0 us -> 124 us
  matrix products: 55.4 us -> 0 us
  other arithmetic: 19.3 us -> 0 us
  between operations: 14.4 us -> 0.66 us
    all_gather x5 -> x0, waiting for transfers between devices: 460 us -> none  [the longest x1 119 us: on_device(): lax.all_gather(image_in, 'tp', axis=0, tiled=True)]
    reduce_scatter x2 -> x0, waiting for transfers between devices: 448 us -> none  [the longest x1 235 us: on_device(): lax.psum_scatter(jnp.dot(block, image_merge, preferred_element_type=jnp.f...]
    pallas_call x0 -> x1, Pallas kernels: none -> 124 us  [on_device(): pl.pallas_call(kernel, out_shape=(jax.ShapeDtypeStruct((ROWS, D), BF16),...]
    dot_general x38 -> x0, matrix products: 55.4 us -> none  [the longest x17 23.4 us: attend_block(): jnp.einsum('hqk,khd->hqd', weights.astype(jnp.bfloat16), value_block, pre...]
  transfers between devices with their start and end apart: 7 -> 0, of which waited for: 7 -> 0; matrix products, arithmetic and copies ran while one was open for 2% -> 0% of each run, Pallas kernels for 0% -> 0%
where the time goes in v1:
time: 135 us
  Pallas kernels  124 us (92%)
  local copies, waits for them, and re-layouts  9.97 us (7%)
    pallas_call x1, Pallas kernels, on_device(): pl.pallas_call(kernel, out_shape=(jax.ShapeDtypeStruct((ROWS, D), BF16),...  124 us
    unnamed x19, local copies, waits for them, and re-layouts  9.97 us

profile of v1, /device:TPU:2, one launch (start us, length us, event | category | flops | bytes accessed | tf_op | source)
XLA Modules:
  0.0 134.6 jit_solution(528123907221311291)
XLA Ops:
  0.6 0.9 copy.11.wtm
  1.5 0.0 copy-start
  1.5 1.7 %copy-done = bf16[3072,384]{1,0:T(8,128)(2,1)S(1)} copy-done((bf16[3072,384]{1,0:T(8,128)(2,1)S(1)}, bf16[3072,384]{1,0:T(8,128)(2,1)}, u32[]{:S(2)}) %copy-start) | copy-done | bytes 2359320
  3.2 0.0 copy-start.1
  3.2 1.1 copy-done.1
  4.3 0.0 copy-start.2
  4.3 0.9 copy-done.2
  5.3 0.0 copy-start.3
  5.3 0.9 copy-done.3
  6.2 0.0 copy-start.4
  6.2 0.9 copy-done.4
  7.1 0.0 copy-start.5
  7.1 0.8 copy-done.5
  7.9 0.0 copy-start.6
  7.9 0.8 copy-done.6
  8.7 0.0 copy-start.7
  8.7 0.7 copy-done.7
  9.3 123.9 %joint_attention.1 = (bf16[32,3072]{1,0:T(8,128)(2,1)S(1)}, bf16[16,192]{1,0:T(8,128)(2,1)S(1)}) custom-call(bf16[32,3072]{1,0:T(8,128)(2,1)S(1)} %copy-done.2, bf16[16,3072]{1,0:T(8,128)(2,1)S(1)} %copy-done.4, f32[3,3072]{1,0:T(4,128)S(1)} %copy-done.5, f32[3,3072]{1,0:T(4,128)S(1)} %copy-done.6, bf16[3072,384]{1,0:T(8,128)(2,1)S(1)} %copy-done, ...), custom_call_target="tpu_custom_call" | custom-call | flops 7000000000 | bytes 8000000 | tf_op jit(solution)/shard_map/joint_attention/pallas_call | solution.py:452
  133.3 0.7 copy.14
  134.0 0.6 copy.15
Async XLA Ops:
  1.5 1.7 %copy-start = (bf16[3072,384]{1,0:T(8,128)(2,1)S(1)}, bf16[3072,384]{1,0:T(8,128)(2,1)}, u32[]{:S(2)}) copy-start(bf16[3072,384]{1,0:T(8,128)(2,1)} %wp_in.1) | copy-start | bytes 7077892
  3.2 1.1 copy-start.1
  4.3 0.9 copy-start.2
  5.3 0.9 copy-start.3
  6.2 0.9 copy-start.4
  7.1 0.8 copy-start.5
  7.9 0.8 copy-start.6
  8.7 0.7 copy-start.7

commit v2 on v0

v2 whole, which is shorter than its diff:
```python
import jax
import jax.numpy as jnp
from jax import lax
from jax.experimental import pallas as pl
from jax.experimental.pallas import tpu as pltpu
from jax.sharding import PartitionSpec as P

HEAD_DIM = 128
D = 3072
EPS = 1e-06
DW = D + 128
NX, NZ, NY, NCTX, NTP = 4, 4, 8, 16, 16
ROWS = 32
TROWS = 16
CHUNKS = (
    ((0, 0), (1, 0), (7, 0)),
    ((2, 0), (6, 0), (0, 1)),
    ((3, 0), (5, 0), (4, 0)),
    ((1, 1), (7, 1)),
    ((2, 1), (6, 1)),
    ((3, 1), (5, 1)),
    ((4, 1),),
)
COUNT = tuple(32 * len(members) for members in CHUNKS)
START = tuple(sum(COUNT[:c]) for c in range(len(CHUNKS)))
NCH = len(CHUNKS)
RING = ((0,), (1, 7), (2, 6), (3, 5), (4,))
RSTART = (0, 32, 96, 160, 224)
RCOUNT = (32, 64, 64, 64, 32)
NQ = 512 + TROWS
F32, BF16 = jnp.float32, jnp.bfloat16
LOG2E = 1.4426950408889634


def offset(r, h):
    for c, members in enumerate(CHUNKS):
        if (r, h) in members:
            return START[c] + members.index((r, h)) * ROWS


def layer_norm(tokens, modulation):
    tokens = tokens.astype(F32)
    centred = tokens - jnp.mean(tokens, axis=1, keepdims=True)
    scaled = centred * lax.rsqrt(jnp.mean(centred * centred, axis=1, keepdims=True) + EPS)
    return (scaled * (1.0 + modulation[1:2]) + modulation[0:1]).astype(BF16)


def head_norm(features, gain):
    normed = features * lax.rsqrt(jnp.mean(features * features, axis=1, keepdims=True) + EPS)
    return (normed * gain).astype(BF16)


def arrived(ref, sem):
    pltpu.make_async_copy(ref, ref, sem).wait()


def kernel(
    img_in, txt_in, imod_in, tmod_in, wp_in, wt_in, wm_in, wtm_in, gains_in,
    out_i, out_t,
    img, txt, imod, tmod, wt, wtm, gains,
    g, gm, wp, w2, kv, kvt, q, tf, tpart, trcv, best_s, total_s, acc_s, o, ox, to, top, tfar, tor, rr, rl, sr, sl,
    local_sem, a_send, a_recv, z_send, z_recv, x_send, x_recv,
    tp_send, tp_recv, tk_send, tk_recv, to_send, to_recv, tm_send, tm_recv, far_send, far_recv,
    w_send, w_recv, o_send, o_recv, r_send, r_recv,
):
    ctx, tp, dp = lax.axis_index("ctx"), lax.axis_index("tp"), lax.axis_index("dp")
    x, z = lax.rem(ctx, NX), lax.div(ctx, NX)
    y, hi = lax.rem(tp, NY), lax.div(tp, NY)
    mirror_ctx = (NZ - 1 - z) * NX + x
    mirror = {"ctx": mirror_ctx, "tp": lax.rem(tp + NY, NTP)}
    far = {"tp": lax.rem(tp + NY, NTP)}
    y_left = {"tp": hi * NY + lax.rem(y + NY - 1, NY)}
    y_right = {"tp": hi * NY + lax.rem(y + 1, NY)}
    x_left = {"ctx": z * NX + lax.rem(x + NX - 1, NX)}
    x_right = {"ctx": z * NX + lax.rem(x + 1, NX)}
    other_core = {"dp": 1 - dp}
    def start(src, dst, ss, rs, device):
        pltpu.make_async_remote_copy(
            src_ref=src, dst_ref=dst, send_sem=ss, recv_sem=rs,
            device_id=device, device_id_type=pl.DeviceIdType.MESH,
        ).start()

    def ctx_peers(act):
        def step(i, carry):
            act(lax.rem(ctx + i, NCTX))
            return carry

        lax.fori_loop(1, NCTX, step, 0)

    barrier = pltpu.get_barrier_semaphore()

    def greet(device):
        pl.semaphore_signal(barrier, inc=1, device_id=device, device_id_type=pl.DeviceIdType.MESH)

    greet(mirror)
    greet(far)
    ctx_peers(lambda i: greet({"ctx": i}))
    for i in range(1, NY):
        greet({"tp": hi * NY + lax.rem(y + i, NY)})
    greet(other_core)

    loads = []
    wanted = (
        (img_in, img), (txt_in, txt), (imod_in, imod), (tmod_in, tmod), (gains_in, gains),
        (wp_in, wp), (wt_in, wt.at[pl.ds(0, 192)]), (wm_in, w2.at[pl.ds(0, HEAD_DIM)]), (wtm_in, wtm),
    )
    for i, (src, dst) in enumerate(wanted):
        loads.append(pltpu.make_async_copy(src, dst, local_sem.at[i]))
        loads[-1].start()
    for i in range(4):
        loads[i].wait()
    wt[192:256, :] = jnp.zeros((64, 384), BF16)

    normed = layer_norm(img[...], imod[...])
    g[0:ROWS, 0:D] = normed
    gm[:, 0:D] = normed
    tf[...] = layer_norm(txt[...], tmod[...]).astype(F32)

    def columns_of(ref, rows, who):
        base = pl.multiple_of(lax.div(who * 3, 2) * 128, 128)
        wide = ref[rows, pl.ds(base, 256)]
        return jnp.where(lax.rem(who, 2) == 1, pltpu.roll(wide, 192, 1), wide)

    for ref, who in ((g, ctx), (gm, mirror_ctx)):
        columns = columns_of(tf, slice(0, TROWS), who).astype(BF16)
        ref[0:16, D:DW] = columns[:, 0:128]
        ref[16:32, D:DW] = columns[:, 128:256]

    pl.semaphore_wait(barrier, (NCTX - 1) + (NY - 1) + 3)

    def rows_of(r, h, p):
        return g.at[pl.ds(offset(r, h) + p * 16, 16)]

    def forward(r, h, side, p):
        there = r + 1 if side == 0 else (r + NY - 1) % NY
        if there == 4 and p != side:
            return
        start(
            rows_of(r, h, p), rows_of(there, h, p), a_send, a_recv.at[there, h, p],
            y_left if side == 0 else y_right,
        )

    for p in (0, 1):
        start(gm.at[pl.ds(p * 16, 16)], rows_of(0, 1, p), a_send, a_recv.at[0, 1, p], mirror)
        forward(0, 0, 0, p)
        forward(0, 0, 1, p)

    def tokens(r, h, p):
        if r == 0:
            arrived(rows_of(0, h, p), a_recv.at[0, h, p])
            forward(0, h, 0, p)
            forward(0, h, 1, p)
        elif r == 4:
            arrived(rows_of(4, h, p), a_recv.at[4, h, p])
        else:
            arrived(rows_of(r, h, p), a_recv.at[r, h, p])
            forward(r, h, 0, p)
            arrived(rows_of(NY - r, h, p), a_recv.at[NY - r, h, p])
            forward(NY - r, h, 1, p)

    def gain(i):
        return gains[i : i + 1, :]

    def project(c):
        rows = pl.ds(START[c], COUNT[c])
        out = jnp.dot(g[rows, 0:D], wp[...], preferred_element_type=F32)
        q[rows, :] = head_norm(out[:, 0:128], gain(0))
        kv[0, rows, 0:128] = head_norm(out[:, 128:256], gain(1))
        kv[0, rows, 128:256] = out[:, 256:384].astype(BF16)

    def text_project(c):
        blocks = COUNT[c] // ROWS
        columns = g[pl.ds(START[c], COUNT[c]), D:DW].reshape(blocks, 2, 16, 128)
        columns = jnp.concatenate([columns[:, 0], columns[:, 1]], axis=2).reshape(blocks * 16, 256)
        out = jnp.dot(columns, wt[...], preferred_element_type=F32)
        for b, (r, h) in enumerate(CHUNKS[c]):
            slot = r * 2 + h
            tpart[slot] = out[b * 16 : b * 16 + 16].astype(BF16)
            target = lax.rem(h + hi, 2) * NY + lax.rem(y + r, NY)

            @pl.when(target != ctx)
            def _():
                start(tpart.at[slot], trcv.at[ctx], tp_send, tp_recv, {"ctx": target})

    def kv_rows(k, r, c, part=None):
        count = COUNT[c] if part is None else COUNT[c] // 2
        return kv.at[k * NX + r, pl.ds(START[c] + (0 if part is None else part * count), count)]

    def send_x(c, k):
        start(kv_rows(k, 0, c), kv_rows(k, 1, c), x_send, x_recv.at[c, k, 0], x_left)
        start(kv_rows(k, 0, c), kv_rows(k, 3, c), x_send, x_recv.at[c, k, 1], x_right)

    def spread(c):
        for k in (1, 3, 2):
            device = {"ctx": lax.rem(z + k, NZ) * NX + x}
            start(kv_rows(0, 0, c), kv_rows(NZ - k, 0, c), z_send, z_recv.at[c, NZ - k], device)
        send_x(c, 0)

    def across(c, k):
        arrived(kv_rows(k, 0, c), z_recv.at[c, k])
        send_x(c, k)

    def around(c, k):
        arrived(kv_rows(k, 1, c), x_recv.at[c, k, 0])
        start(kv_rows(k, 1, c, 0), kv_rows(k, 2, c, 0), x_send, x_recv.at[c, k, 2], x_left)
        arrived(kv_rows(k, 3, c), x_recv.at[c, k, 1])
        start(kv_rows(k, 3, c, 1), kv_rows(k, 2, c, 1), x_send, x_recv.at[c, k, 2], x_right)

    def complete(c):
        for k in range(NZ):
            arrived(kv_rows(k, 2, c), x_recv.at[c, k, 2])

    piece = x * 2 + dp

    def merge_piece(p):
        return w2.at[pl.ds(pl.multiple_of(HEAD_DIM + p * 16, 16), 16)]

    def merge_weights(step):
        if step == 0:
            loads[7].wait()
            start(w2.at[pl.ds(pl.multiple_of(piece * 16, 16), 16)], merge_piece(piece), w_send, w_recv.at[0], mirror)
        elif step == 1:
            arrived(merge_piece(piece), w_recv.at[0])
            for i in range(1, NX):
                start(
                    merge_piece(piece), merge_piece(piece), w_send, w_recv.at[1],
                    {"ctx": z * NX + lax.rem(x + i, NX)},
                )
        elif step == 2:
            arrived(w2.at[pl.ds(0, 48)], w_recv.at[1])
            for i in range(NX):
                p = i * 2 + dp
                start(merge_piece(p), merge_piece(p), w_send, w_recv.at[2], other_core)
        else:
            arrived(w2.at[pl.ds(0, 64)], w_recv.at[2])

    def text_rows(i):
        return kvt.at[pl.ds(pl.multiple_of(i * TROWS, TROWS), TROWS)]

    def text_heads():
        arrived(trcv.at[pl.ds(0, NCTX - 1)], tp_recv)
        own = lax.rem(lax.rem(ctx, NY) + NY - y, NY) * 2 + lax.rem(lax.div(ctx, NY) + hi, 2)
        trcv[ctx] = tpart[own]
        total = jnp.sum(trcv[...].astype(F32), axis=0)
        q[512:NQ, :] = head_norm(total[:, 0:128], gain(2))
        mine = pl.ds(pl.multiple_of(ctx * TROWS, TROWS), TROWS)
        kvt[mine, 0:128] = head_norm(total[:, 128:256], gain(3))
        kvt[mine, 128:256] = total[:, 256:384].astype(BF16)
        ctx_peers(lambda i: start(text_rows(ctx), text_rows(ctx), tk_send, tk_recv, {"ctx": i}))

    scale = HEAD_DIM**-0.5 * LOG2E

    def fold(state, query, key_blocks):
        best, total, weighted = state
        for both in key_blocks:
            s = lax.dot_general(query, both[:, 0:128], (((1,), (1,)), ((), ())), preferred_element_type=F32)
            fresh = jnp.maximum(best, jnp.max(s, axis=1, keepdims=True))
            decay = jnp.exp2((best - fresh) * scale)
            weights = jnp.exp2((s - fresh) * scale)
            total = total * decay + jnp.sum(weights, axis=1, keepdims=True)
            weighted = weighted * decay + jnp.dot(weights.astype(BF16), both[:, 128:256], preferred_element_type=F32)
            best = fresh
        return best, total, weighted

    def attend(first, end, low, high):
        rows = pl.ds(first, end - first)
        count = START[high] + COUNT[high] - START[low]
        both = kv[:, pl.ds(START[low], count)].reshape(NCTX * count, 256)
        state = fold((best_s[rows, :], total_s[rows, :], acc_s[rows, :]), q[rows, :], [both])
        best_s[rows, :], total_s[rows, :], acc_s[rows, :] = state

    def finish(c):
        first = RING[c][0]
        ranges = [(offset(first, h), RCOUNT[c]) for h in (0, 1)]
        if c == 4:
            ranges.append((512, TROWS))

        def rows_from(ref):
            return jnp.concatenate([ref[pl.ds(at, n), :] for at, n in ranges], axis=0)

        last = kv[:, pl.ds(START[NCH - 1], COUNT[NCH - 1])].reshape(NCTX * COUNT[NCH - 1], 256)
        state = (rows_from(best_s), rows_from(total_s), rows_from(acc_s))
        best, total, weighted = fold(state, rows_from(q), [last, kvt[...]])
        return (weighted / total).astype(BF16)

    best_s[...] = jnp.full((NQ, 1), -1e30, F32)
    total_s[...] = jnp.zeros((NQ, 1), F32)
    acc_s[...] = jnp.zeros((NQ, HEAD_DIM), F32)

    def enter(c):
        project(c)
        spread(c)
        text_project(c)

    tokens(1, 0, 0)
    tokens(1, 0, 1)
    for i in (4, 5, 6):
        loads[i].wait()
    enter(0)
    tokens(0, 1, 0)
    tokens(2, 0, 0)
    tokens(2, 0, 1)
    around(0, 0)
    tokens(0, 1, 1)
    enter(1)
    tokens(1, 1, 0)
    across(0, 3)
    merge_weights(0)
    across(0, 1)
    tokens(3, 0, 0)
    across(0, 2)
    around(1, 0)
    tokens(3, 0, 1)
    around(0, 3)
    across(1, 3)
    around(0, 1)
    across(1, 1)
    tokens(1, 1, 1)
    enter(3)
    around(0, 2)
    across(1, 2)
    around(1, 3)
    tokens(2, 1, 0)
    merge_weights(1)
    around(1, 1)
    tokens(4, 0, 0)
    tokens(4, 0, 1)
    enter(2)
    around(1, 2)
    around(3, 0)
    across(3, 1)
    across(3, 3)
    complete(0)
    tokens(2, 1, 1)
    enter(4)
    across(3, 2)
    merge_weights(2)
    tokens(3, 1, 0)
    around(2, 0)
    complete(1)
    attend(0, 288, 0, 1)
    tokens(3, 1, 1)
    enter(5)
    around(3, 1)
    around(3, 3)
    around(3, 2)
    around(4, 0)
    across(2, 1)
    tokens(4, 1, 0)
    tokens(4, 1, 1)
    enter(6)
    across(2, 3)
    across(2, 2)
    across(4, 3)
    attend(288, 512, 0, 1)
    around(5, 0)
    across(4, 1)
    across(4, 2)
    complete(3)
    around(2, 1)
    across(5, 3)
    around(6, 0)
    across(5, 1)
    around(2, 3)
    across(5, 2)
    around(2, 2)
    across(6, 3)
    around(4, 3)
    across(6, 1)
    across(6, 2)
    around(4, 1)
    around(4, 2)
    text_heads()
    around(5, 3)
    around(5, 1)
    around(5, 2)
    complete(2)
    attend(0, 512, 2, 2)
    around(6, 1)
    around(6, 3)
    around(6, 2)
    attend(512, 528, 0, 2)
    complete(4)
    attend(0, 528, 3, 4)
    complete(5)
    complete(6)
    attend(0, 528, 5, 5)
    arrived(kvt.at[pl.ds(0, (NCTX - 1) * TROWS)], tk_recv)
    merge_weights(3)

    def exchange(c):
        half = RCOUNT[c]
        rows = pl.ds(RSTART[c], half)
        mixed = finish(c)
        ox[rows, :] = mixed[half : 2 * half]
        start(ox.at[rows], o.at[rows, pl.ds(128, 128)], o_send, o_recv.at[c], mirror)
        o[rows, 0:128] = mixed[0:half]
        if c == 4:
            to[ctx] = mixed[2 * half :]
            ctx_peers(lambda i: start(to.at[ctx], to.at[ctx], to_send, to_recv, {"ctx": i}))

    def text_merge(step):
        if step == 0:
            arrived(to.at[pl.ds(0, NCTX - 1)], to_recv)
            loads[8].wait()
            part = lax.dot_general(
                to[...].reshape(NCTX * TROWS, HEAD_DIM), wtm[...], (((1,), (1,)), ((), ())), preferred_element_type=F32
            )
            top[:, :, 0:192] = part.reshape(NTP, TROWS, 192).astype(BF16)
            top[:, :, 192:256] = jnp.zeros((NTP, TROWS, 64), BF16)
            start(top.at[pl.ds((1 - hi) * NY, NY)], tfar, far_send, far_recv, far)
        elif step == 1:
            arrived(tfar, far_recv)
            tfar[...] = (tfar[...].astype(F32) + top[pl.ds(hi * NY, NY)].astype(F32)).astype(BF16)
            for i in range(1, NY):
                there = lax.rem(y + i, NY)
                start(tfar.at[there], tor.at[i], tm_send, tm_recv, {"tp": hi * NY + there})
        else:
            arrived(tor.at[pl.ds(1, NY - 1)], tm_recv)
            tor[0] = tfar[y]
            text_total = jnp.sum(tor[...].astype(F32), axis=0)[:, 0:192]
            tf[0:3, :] = tmod[...]
            gate = columns_of(tf, slice(2, 3), ctx)[:, 0:192]
            out_t[...] = (gate * text_total).astype(BF16)

    def merge(c):
        rows = pl.ds(RSTART[c], RCOUNT[c])
        arrived(o.at[rows, pl.ds(128, 128)], o_recv.at[c])
        return jnp.dot(o[rows, :], w2[...], preferred_element_type=F32)

    def reduce(c):
        part = merge(c)
        if c == 0:
            total = part
            for p in (0, 1):
                half = slice(p * 16, p * 16 + 16)
                for way, recv in enumerate((rr, rl)):
                    arrived(recv.at[0, pl.ds(p * 16, 16)], r_recv.at[way, 0, p])
                sums = part[half] + rr[0, half, :].astype(F32) + rl[0, half, :].astype(F32)
                out_i[half, :] = (imod[2:3, :] * sums).astype(BF16)
            return
        for turn in (0, 1):
            for way, recv, out, device in ((0, rr, sr, y_right), (1, rl, sl, y_left)):
                p = 1 - way if turn == 0 else way
                half = slice(p * 16, p * 16 + 16)
                ref = pl.ds(p * 16, 16)
                if c == 4:
                    if p != way:
                        continue
                    sums = part[half]
                else:
                    sums = part[way * ROWS + p * 16 : way * ROWS + p * 16 + 16]
                    if c < 3 or p == way:
                        arrived(recv.at[c, ref], r_recv.at[way, c, p])
                        sums = sums + recv[c, half, :].astype(F32)
                out[c - 1, half, :] = sums.astype(BF16)
                start(out.at[c - 1, ref], recv.at[c - 1, ref], r_send, r_recv.at[way, c - 1, p], device)

    exchange(4)
    exchange(3)
    reduce(4)
    exchange(2)
    reduce(3)
    text_merge(0)
    exchange(1)
    reduce(2)
    exchange(0)
    text_merge(1)
    reduce(1)
    text_merge(2)
    reduce(0)

    arrived(g.at[pl.ds(0, 480)], a_send)
    arrived(kv.at[pl.ds(0, 3)], z_send)
    arrived(kv.at[pl.ds(0, 12)], x_send)
    arrived(tpart.at[pl.ds(0, NCTX - 1)], tp_send)
    arrived(kvt.at[pl.ds(0, (NCTX - 1) * TROWS)], tk_send)
    arrived(to.at[pl.ds(0, NCTX - 1)], to_send)
    arrived(tfar, far_send)
    arrived(tor.at[pl.ds(0, NY - 1)], tm_send)
    arrived(w2.at[pl.ds(0, 128)], w_send)
    arrived(ox, o_send)
    arrived(w2.at[pl.ds(0, 224)], r_send)


def on_device(*arrays):
    arrays = arrays[:7] + (arrays[7].T,) + arrays[8:]
    dma = pltpu.SemaphoreType.DMA
    vmem = pl.BlockSpec(memory_space=pltpu.VMEM)
    hbm = pl.BlockSpec(memory_space=pltpu.HBM)
    return pl.pallas_call(
        kernel,
        out_shape=(
            jax.ShapeDtypeStruct((ROWS, D), BF16),
            jax.ShapeDtypeStruct((TROWS, 192), BF16),
        ),
        in_specs=[hbm] * 9,
        out_specs=(vmem, vmem),
        scratch_shapes=[
            pltpu.VMEM((ROWS, D), BF16),
            pltpu.VMEM((TROWS, D), BF16),
            pltpu.VMEM((3, D), F32),
            pltpu.VMEM((3, D), F32),
            pltpu.VMEM((256, 384), BF16),
            pltpu.VMEM((192, HEAD_DIM), BF16),
            pltpu.VMEM((4, HEAD_DIM), F32),
            pltpu.VMEM((512, DW), BF16),
            pltpu.VMEM((ROWS, DW), BF16),
            pltpu.VMEM((D, 384), BF16),
            pltpu.VMEM((256, D), BF16),
            pltpu.VMEM((NCTX, 512, 256), BF16),
            pltpu.VMEM((NCTX * TROWS, 256), BF16),
            pltpu.VMEM((NQ, HEAD_DIM), BF16),
            pltpu.VMEM((TROWS, D), F32),
            pltpu.VMEM((NTP, TROWS, 384), BF16),
            pltpu.VMEM((NCTX, TROWS, 384), BF16),
            pltpu.VMEM((NQ, 1), F32),
            pltpu.VMEM((NQ, 1), F32),
            pltpu.VMEM((NQ, HEAD_DIM), F32),
            pltpu.VMEM((256, 256), BF16),
            pltpu.VMEM((256, HEAD_DIM), BF16),
            pltpu.VMEM((NCTX, TROWS, HEAD_DIM), BF16),
            pltpu.VMEM((NTP, TROWS, 256), BF16),
            pltpu.VMEM((NY, TROWS, 256), BF16),
            pltpu.VMEM((NY, TROWS, 256), BF16),
            pltpu.VMEM((4, ROWS, D), BF16),
            pltpu.VMEM((4, ROWS, D), BF16),
            pltpu.VMEM((4, ROWS, D), BF16),
            pltpu.VMEM((4, ROWS, D), BF16),
            dma((9,)),
            dma,
            dma((NY, 2, 2)),
            dma,
            dma((NCH, NZ)),
            dma,
            dma((NCH, NZ, 3)),
            dma, dma,
            dma, dma,
            dma, dma,
            dma, dma,
            dma, dma,
            dma, dma((3,)),
            dma, dma((5,)),
            dma, dma((2, 4, 2)),
        ],
        compiler_params=pltpu.CompilerParams(
            collective_id=0, has_side_effects=True, vmem_limit_bytes=63 * 1024 * 1024
        ),
        cost_estimate=pl.CostEstimate(flops=7_000_000_000, bytes_accessed=8_000_000, transcendentals=4_500_000),
        name="joint_attention",
    )(*arrays)


def solution(mesh):
    placed = (
        P(("dp", "ctx", "tp"), None),
        P(("dp", "tp"), None),
        P("dp", None),
        P("dp", None),
        P(None, "tp"),
        P("ctx", "tp"),
        P("tp", None),
        P("tp", "ctx"),
        P(),
    )
    return jax.shard_map(
        on_device,
        mesh=mesh,
        in_specs=placed,
        out_specs=(P(("dp", "ctx", "tp"), None), P(("dp", "tp"), "ctx")),
        check_vma=False,
    )
```

time: 1000 us -> 103 us (0.10)
  the two profiles are of different devices: /device:TPU:2 before, /device:TPU:8 now
where the time goes in v2:
time: 103 us
  Pallas kernels  99.6 us (97%)
  local copies, waits for them, and re-layouts  2.91 us (3%)
    pallas_call x1, Pallas kernels, on_device(): pl.pallas_call(kernel, out_shape=(jax.ShapeDtypeStruct((ROWS, D), BF16),...  99.6 us
    unnamed x2, local copies, waits for them, and re-layouts  2.91 us

profile of v2, /device:TPU:8, one launch (start us, length us, event | category | flops | bytes accessed | tf_op | source)
XLA Modules:
  0.0 103.2 jit_solution(12782041664937255679)
XLA Ops:
  0.6 99.6 %joint_attention.1 = (bf16[32,3072]{1,0:T(8,128)(2,1)}, bf16[16,192]{1,0:T(8,128)(2,1)}) custom-call(bf16[32,3072]{1,0:T(8,128)(2,1)} %img_in.1, bf16[16,3072]{1,0:T(8,128)(2,1)} %txt_in.1, f32[3,3072]{1,0:T(4,128)} %imod_in.1, f32[3,3072]{1,0:T(4,128)} %tmod_in.1, bf16[3072,384]{1,0:T(8,128)(2,1)} %wp_in.1, bf16[192,384]{1,0:T(8,128)(2,1)} %wt_in.1, ...), custom_call_target="tpu_custom_call" | custom-call | flops 7000000000 | bytes 8000000 | tf_op jit(solution)/shard_map/joint_attention/pallas_call | solution.py:491
  100.3 1.6 %copy.13 = bf16[32,3072]{1,0:T(8,128)(2,1)} copy(bf16[32,3072]{1,0:T(8,128)(2,1)} %get-tuple-element.4) | data formatting | bytes 393216
  101.9 1.3 %copy.14 = bf16[16,192]{1,0:T(8,128)(2,1)} copy(bf16[16,192]{1,0:T(8,128)(2,1)} %get-tuple-element.5) | data formatting | bytes 12288

commit v3 on v2

--- a/solution.py
+++ b/solution.py
@@ -8,16 +8,17 @@
 HEAD_DIM = 128
 D = 3072
 EPS = 1e-06
+HALF = D // 2
 DW = D + 128
 NX, NZ, NY, NCTX, NTP = 4, 4, 8, 16, 16
 ROWS = 32
 TROWS = 16
 CHUNKS = (
     ((0, 0), (1, 0), (7, 0)),
-    ((2, 0), (6, 0), (0, 1)),
-    ((3, 0), (5, 0), (4, 0)),
+    ((2, 0), (6, 0)),
+    ((0, 1), (3, 0), (5, 0)),
     ((1, 1), (7, 1)),
-    ((2, 1), (6, 1)),
+    ((4, 0), (2, 1), (6, 1)),
     ((3, 1), (5, 1)),
     ((4, 1),),
 )
@@ -58,9 +59,9 @@
     img_in, txt_in, imod_in, tmod_in, wp_in, wt_in, wm_in, wtm_in, gains_in,
     out_i, out_t,
     img, txt, imod, tmod, wt, wtm, gains,
-    g, gm, wp, w2, kv, kvt, q, tf, tpart, trcv, best_s, total_s, acc_s, o, ox, to, top, tfar, tor, rr, rl, sr, sl,
+    g, gm, wp, w2, kv, kvt, q, tf, tpart, trcv, best_s, total_s, acc_s, o, ox, to, top, tor, rr, rl, sr, sl,
     local_sem, a_send, a_recv, z_send, z_recv, x_send, x_recv,
-    tp_send, tp_recv, tk_send, tk_recv, to_send, to_recv, tm_send, tm_recv, far_send, far_recv,
+    tp_send, tp_recv, tk_send, tk_recv, to_send, to_recv, tm_send, tm_recv, far_in,
     w_send, w_recv, o_send, o_recv, r_send, r_recv,
 ):
     ctx, tp, dp = lax.axis_index("ctx"), lax.axis_index("tp"), lax.axis_index("dp")
@@ -73,6 +74,7 @@
     y_right = {"tp": hi * NY + lax.rem(y + 1, NY)}
     x_left = {"ctx": z * NX + lax.rem(x + NX - 1, NX)}
     x_right = {"ctx": z * NX + lax.rem(x + 1, NX)}
+    x_opposite = {"ctx": z * NX + lax.rem(x + 2, NX)}
     other_core = {"dp": 1 - dp}
     def start(src, dst, ss, rs, device):
         pltpu.make_async_remote_copy(
@@ -127,6 +129,7 @@
         ref[16:32, D:DW] = columns[:, 128:256]
 
     pl.semaphore_wait(barrier, (NCTX - 1) + (NY - 1) + 3)
+    pl.semaphore_signal(far_in, inc=1, device_id=far, device_id_type=pl.DeviceIdType.MESH)
 
     def rows_of(r, h, p):
         return g.at[pl.ds(offset(r, h) + p * 16, 16)]
@@ -189,6 +192,8 @@
     def send_x(c, k):
         start(kv_rows(k, 0, c), kv_rows(k, 1, c), x_send, x_recv.at[c, k, 0], x_left)
         start(kv_rows(k, 0, c), kv_rows(k, 3, c), x_send, x_recv.at[c, k, 1], x_right)
+        if c == NCH - 1:
+            start(kv_rows(k, 0, c), kv_rows(k, 2, c), x_send, x_recv.at[c, k, 2], x_opposite)
 
     def spread(c):
         for k in (1, 3, 2):
@@ -202,6 +207,9 @@
 
     def around(c, k):
         arrived(kv_rows(k, 1, c), x_recv.at[c, k, 0])
+        if c == NCH - 1:
+            arrived(kv_rows(k, 3, c), x_recv.at[c, k, 1])
+            return
         start(kv_rows(k, 1, c, 0), kv_rows(k, 2, c, 0), x_send, x_recv.at[c, k, 2], x_left)
         arrived(kv_rows(k, 3, c), x_recv.at[c, k, 1])
         start(kv_rows(k, 3, c, 1), kv_rows(k, 2, c, 1), x_send, x_recv.at[c, k, 2], x_right)
@@ -210,29 +218,18 @@
         for k in range(NZ):
             arrived(kv_rows(k, 2, c), x_recv.at[c, k, 2])
 
-    piece = x * 2 + dp
-
-    def merge_piece(p):
-        return w2.at[pl.ds(pl.multiple_of(HEAD_DIM + p * 16, 16), 16)]
+    def merge_half(core):
+        return w2.at[pl.ds(pl.multiple_of(HEAD_DIM + core * 64, 64), 64)]
 
     def merge_weights(step):
         if step == 0:
             loads[7].wait()
-            start(w2.at[pl.ds(pl.multiple_of(piece * 16, 16), 16)], merge_piece(piece), w_send, w_recv.at[0], mirror)
+            start(w2.at[pl.ds(pl.multiple_of(dp * 64, 64), 64)], merge_half(dp), w_send, w_recv.at[0], mirror)
         elif step == 1:
-            arrived(merge_piece(piece), w_recv.at[0])
-            for i in range(1, NX):
-                start(
-                    merge_piece(piece), merge_piece(piece), w_send, w_recv.at[1],
-                    {"ctx": z * NX + lax.rem(x + i, NX)},
-                )
-        elif step == 2:
-            arrived(w2.at[pl.ds(0, 48)], w_recv.at[1])
-            for i in range(NX):
-                p = i * 2 + dp
-                start(merge_piece(p), merge_piece(p), w_send, w_recv.at[2], other_core)
+            arrived(merge_half(dp), w_recv.at[0])
+            start(merge_half(dp), merge_half(dp), w_send, w_recv.at[1], other_core)
         else:
-            arrived(w2.at[pl.ds(0, 64)], w_recv.at[2])
+            arrived(merge_half(1 - dp), w_recv.at[1])
 
     def text_rows(i):
         return kvt.at[pl.ds(pl.multiple_of(i * TROWS, TROWS), TROWS)]
@@ -269,7 +266,7 @@
         state = fold((best_s[rows, :], total_s[rows, :], acc_s[rows, :]), q[rows, :], [both])
         best_s[rows, :], total_s[rows, :], acc_s[rows, :] = state
 
-    def finish(c):
+    def finish(c, low):
         first = RING[c][0]
         ranges = [(offset(first, h), RCOUNT[c]) for h in (0, 1)]
         if c == 4:
@@ -278,7 +275,8 @@
         def rows_from(ref):
             return jnp.concatenate([ref[pl.ds(at, n), :] for at, n in ranges], axis=0)
 
-        last = kv[:, pl.ds(START[NCH - 1], COUNT[NCH - 1])].reshape(NCTX * COUNT[NCH - 1], 256)
+        count = START[-1] + COUNT[-1] - START[low]
+        last = kv[:, pl.ds(START[low], count)].reshape(NCTX * count, 256)
         state = (rows_from(best_s), rows_from(total_s), rows_from(acc_s))
         best, total, weighted = fold(state, rows_from(q), [last, kvt[...]])
         return (weighted / total).astype(BF16)
@@ -288,110 +286,108 @@
     acc_s[...] = jnp.zeros((NQ, HEAD_DIM), F32)
 
     def enter(c):
+        text_project(c)
         project(c)
         spread(c)
-        text_project(c)
 
     tokens(1, 0, 0)
     tokens(1, 0, 1)
     for i in (4, 5, 6):
         loads[i].wait()
     enter(0)
+    tokens(2, 0, 0)
     tokens(0, 1, 0)
-    tokens(2, 0, 0)
+    around(0, 0)
     tokens(2, 0, 1)
-    around(0, 0)
+    enter(1)
     tokens(0, 1, 1)
-    enter(1)
+    merge_weights(0)
+    across(0, 3)
+    tokens(3, 0, 0)
+    across(0, 1)
+    around(1, 0)
+    across(0, 2)
     tokens(1, 1, 0)
-    across(0, 3)
-    merge_weights(0)
-    across(0, 1)
-    tokens(3, 0, 0)
-    across(0, 2)
-    around(1, 0)
-    tokens(3, 0, 1)
     around(0, 3)
     across(1, 3)
     around(0, 1)
+    tokens(3, 0, 1)
+    enter(2)
+    around(0, 2)
     across(1, 1)
+    across(1, 2)
     tokens(1, 1, 1)
     enter(3)
-    around(0, 2)
-    across(1, 2)
     around(1, 3)
-    tokens(2, 1, 0)
-    merge_weights(1)
-    around(1, 1)
     tokens(4, 0, 0)
     tokens(4, 0, 1)
-    enter(2)
+    around(2, 0)
+    complete(0)
+    across(2, 3)
+    around(1, 1)
+    tokens(2, 1, 0)
     around(1, 2)
+    across(2, 1)
     around(3, 0)
-    across(3, 1)
-    across(3, 3)
-    complete(0)
+    across(2, 2)
     tokens(2, 1, 1)
     enter(4)
+    around(2, 3)
+    across(3, 3)
+    complete(1)
+    attend(0, 256, 0, 1)
+    tokens(3, 1, 0)
+    around(2, 1)
+    across(3, 1)
     across(3, 2)
-    merge_weights(2)
-    tokens(3, 1, 0)
-    around(2, 0)
-    complete(1)
-    attend(0, 288, 0, 1)
+    around(2, 2)
     tokens(3, 1, 1)
     enter(5)
+    around(3, 3)
+    around(4, 0)
+    across(4, 3)
     around(3, 1)
-    around(3, 3)
+    across(4, 1)
+    merge_weights(1)
     around(3, 2)
-    around(4, 0)
-    across(2, 1)
     tokens(4, 1, 0)
     tokens(4, 1, 1)
     enter(6)
-    across(2, 3)
-    across(2, 2)
-    across(4, 3)
-    attend(288, 512, 0, 1)
     around(5, 0)
-    across(4, 1)
     across(4, 2)
+    complete(2)
+    attend(256, 512, 0, 1)
+    across(5, 3)
+    around(4, 3)
+    across(5, 1)
+    across(5, 2)
+    around(4, 1)
     complete(3)
-    around(2, 1)
-    across(5, 3)
+    attend(0, 256, 2, 3)
     around(6, 0)
-    across(5, 1)
-    around(2, 3)
-    across(5, 2)
-    around(2, 2)
+    across(6, 1)
     across(6, 3)
-    around(4, 3)
-    across(6, 1)
     across(6, 2)
-    around(4, 1)
+    attend(256, 512, 2, 3)
+    text_heads()
     around(4, 2)
-    text_heads()
+    around(5, 1)
     around(5, 3)
-    around(5, 1)
+    attend(512, 528, 0, 3)
     around(5, 2)
-    complete(2)
-    attend(0, 512, 2, 2)
     around(6, 1)
     around(6, 3)
     around(6, 2)
-    attend(512, 528, 0, 2)
     complete(4)
-    attend(0, 528, 3, 4)
+    complete(6)
     complete(5)
-    complete(6)
-    attend(0, 528, 5, 5)
     arrived(kvt.at[pl.ds(0, (NCTX - 1) * TROWS)], tk_recv)
-    merge_weights(3)
-
-    def exchange(c):
+    merge_weights(2)
+
+    def exchange(c, low=NCH - 1):
         half = RCOUNT[c]
         rows = pl.ds(RSTART[c], half)
-        mixed = finish(c)
+        mixed = finish(c, low)
         ox[rows, :] = mixed[half : 2 * half]
         start(ox.at[rows], o.at[rows, pl.ds(128, 128)], o_send, o_recv.at[c], mirror)
         o[rows, 0:128] = mixed[0:half]
@@ -408,16 +404,17 @@
             )
             top[:, :, 0:192] = part.reshape(NTP, TROWS, 192).astype(BF16)
             top[:, :, 192:256] = jnp.zeros((NTP, TROWS, 64), BF16)
-            start(top.at[pl.ds((1 - hi) * NY, NY)], tfar, far_send, far_recv, far)
-        elif step == 1:
-            arrived(tfar, far_recv)
-            tfar[...] = (tfar[...].astype(F32) + top[pl.ds(hi * NY, NY)].astype(F32)).astype(BF16)
-            for i in range(1, NY):
-                there = lax.rem(y + i, NY)
-                start(tfar.at[there], tor.at[i], tm_send, tm_recv, {"tp": hi * NY + there})
+            pl.semaphore_wait(far_in, 1)
+
+            def step(i, carry):
+                there = lax.rem(tp + i, NTP)
+                start(top.at[there], tor.at[i], tm_send, tm_recv, {"tp": there})
+                return carry
+
+            lax.fori_loop(1, NTP, step, 0)
         else:
-            arrived(tor.at[pl.ds(1, NY - 1)], tm_recv)
-            tor[0] = tfar[y]
+            arrived(tor.at[pl.ds(1, NTP - 1)], tm_recv)
+            tor[0] = top[tp]
             text_total = jnp.sum(tor[...].astype(F32), axis=0)[:, 0:192]
             tf[0:3, :] = tmod[...]
             gate = columns_of(tf, slice(2, 3), ctx)[:, 0:192]
@@ -430,44 +427,45 @@
 
     def reduce(c):
         part = merge(c)
-        if c == 0:
-            total = part
-            for p in (0, 1):
-                half = slice(p * 16, p * 16 + 16)
-                for way, recv in enumerate((rr, rl)):
-                    arrived(recv.at[0, pl.ds(p * 16, 16)], r_recv.at[way, 0, p])
-                sums = part[half] + rr[0, half, :].astype(F32) + rl[0, half, :].astype(F32)
-                out_i[half, :] = (imod[2:3, :] * sums).astype(BF16)
-            return
         for turn in (0, 1):
-            for way, recv, out, device in ((0, rr, sr, y_right), (1, rl, sl, y_left)):
-                p = 1 - way if turn == 0 else way
-                half = slice(p * 16, p * 16 + 16)
-                ref = pl.ds(p * 16, 16)
-                if c == 4:
-                    if p != way:
-                        continue
-                    sums = part[half]
-                else:
-                    sums = part[way * ROWS + p * 16 : way * ROWS + p * 16 + 16]
-                    if c < 3 or p == way:
-                        arrived(recv.at[c, ref], r_recv.at[way, c, p])
-                        sums = sums + recv[c, half, :].astype(F32)
-                out[c - 1, half, :] = sums.astype(BF16)
-                start(out.at[c - 1, ref], recv.at[c - 1, ref], r_send, r_recv.at[way, c - 1, p], device)
-
-    exchange(4)
+            for j in (0, 1):
+                columns = slice(j * HALF, j * HALF + HALF)
+                if c == 0:
+                    p = turn
+                    half, ref = slice(p * 16, p * 16 + 16), pl.ds(p * 16, 16)
+                    for way, recv in enumerate((rr, rl)):
+                        arrived(recv.at[0, j, ref], r_recv.at[way, 0, p, j])
+                    sums = part[half, columns] + rr[0, j, half, :].astype(F32) + rl[0, j, half, :].astype(F32)
+                    out_i[half, columns] = (imod[2:3, columns] * sums).astype(BF16)
+                    continue
+                for way, recv, out, device in ((0, rr, sr, y_right), (1, rl, sl, y_left)):
+                    p = 1 - way if turn == 0 else way
+                    half, ref = slice(p * 16, p * 16 + 16), pl.ds(p * 16, 16)
+                    if c == 4:
+                        if p != way:
+                            continue
+                        sums = part[half, columns]
+                    else:
+                        first = way * ROWS + p * 16
+                        sums = part[first : first + 16, columns]
+                        if c < 3 or p == way:
+                            arrived(recv.at[c, j, ref], r_recv.at[way, c, p, j])
+                            sums = sums + recv[c, j, half, :].astype(F32)
+                    out[c - 1, j, half, :] = sums.astype(BF16)
+                    start(out.at[c - 1, j, ref], recv.at[c - 1, j, ref], r_send, r_recv.at[way, c - 1, p, j], device)
+
+    exchange(4, 4)
+    attend(0, 528, 4, NCH - 2)
     exchange(3)
     reduce(4)
     exchange(2)
+    text_merge(0)
     reduce(3)
-    text_merge(0)
     exchange(1)
     reduce(2)
     exchange(0)
+    reduce(1)
     text_merge(1)
-    reduce(1)
-    text_merge(2)
     reduce(0)
 
     arrived(g.at[pl.ds(0, 480)], a_send)
@@ -476,8 +474,7 @@
     arrived(tpart.at[pl.ds(0, NCTX - 1)], tp_send)
     arrived(kvt.at[pl.ds(0, (NCTX - 1) * TROWS)], tk_send)
     arrived(to.at[pl.ds(0, NCTX - 1)], to_send)
-    arrived(tfar, far_send)
-    arrived(tor.at[pl.ds(0, NY - 1)], tm_send)
+    arrived(tor.at[pl.ds(0, NTP - 1)], tm_send)
     arrived(w2.at[pl.ds(0, 128)], w_send)
     arrived(ox, o_send)
     arrived(w2.at[pl.ds(0, 224)], r_send)
@@ -521,12 +518,11 @@
             pltpu.VMEM((256, HEAD_DIM), BF16),
             pltpu.VMEM((NCTX, TROWS, HEAD_DIM), BF16),
             pltpu.VMEM((NTP, TROWS, 256), BF16),
-            pltpu.VMEM((NY, TROWS, 256), BF16),
-            pltpu.VMEM((NY, TROWS, 256), BF16),
-            pltpu.VMEM((4, ROWS, D), BF16),
-            pltpu.VMEM((4, ROWS, D), BF16),
-            pltpu.VMEM((4, ROWS, D), BF16),
-            pltpu.VMEM((4, ROWS, D), BF16),
+            pltpu.VMEM((NTP, TROWS, 256), BF16),
+            pltpu.VMEM((4, 2, ROWS, HALF), BF16),
+            pltpu.VMEM((4, 2, ROWS, HALF), BF16),
+            pltpu.VMEM((4, 2, ROWS, HALF), BF16),
+            pltpu.VMEM((4, 2, ROWS, HALF), BF16),
             dma((9,)),
             dma,
             dma((NY, 2, 2)),
@@ -538,10 +534,10 @@
             dma, dma,
             dma, dma,
             dma, dma,
-            dma, dma,
-            dma, dma((3,)),
+            pltpu.SemaphoreType.REGULAR,
+            dma, dma((2,)),
             dma, dma((5,)),
-            dma, dma((2, 4, 2)),
+            dma, dma((2, 4, 2, 2)),
         ],
         compiler_params=pltpu.CompilerParams(
             collective_id=0, has_side_effects=True, vmem_limit_bytes=63 * 1024 * 1024

time: 103 us -> 98.7 us (0.958)
  the two profiles are of different devices: /device:TPU:8 before, /device:TPU:2 now
where the time goes in v3:
time: 98.7 us; the launch traced here: 98.5 us
  Pallas kernels  95 us (96%)
  local copies, waits for them, and re-layouts  2.91 us (3%)
    pallas_call x1, Pallas kernels, on_device(): pl.pallas_call(kernel, out_shape=(jax.ShapeDtypeStruct((ROWS, D), BF16),...  95 us
    unnamed x2, local copies, waits for them, and re-layouts  2.91 us

profile of v3, /device:TPU:2, one launch (start us, length us, event | category | flops | bytes accessed | tf_op | source)
XLA Modules:
  0.0 98.5 jit_solution(8233221544779623224)
XLA Ops:
  0.6 95.0 %joint_attention.1 = (bf16[32,3072]{1,0:T(8,128)(2,1)}, bf16[16,192]{1,0:T(8,128)(2,1)}) custom-call(bf16[32,3072]{1,0:T(8,128)(2,1)} %img_in.1, bf16[16,3072]{1,0:T(8,128)(2,1)} %txt_in.1, f32[3,3072]{1,0:T(4,128)} %imod_in.1, f32[3,3072]{1,0:T(4,128)} %tmod_in.1, bf16[3072,384]{1,0:T(8,128)(2,1)} %wp_in.1, bf16[192,384]{1,0:T(8,128)(2,1)} %wt_in.1, ...), custom_call_target="tpu_custom_call" | custom-call | flops 7000000000 | bytes 8000000 | tf_op jit(solution)/shard_map/joint_attention/pallas_call | solution.py:488
  95.6 1.6 %copy.13 = bf16[32,3072]{1,0:T(8,128)(2,1)} copy(bf16[32,3072]{1,0:T(8,128)(2,1)} %get-tuple-element.4) | data formatting | bytes 393216
  97.2 1.3 %copy.14 = bf16[16,192]{1,0:T(8,128)(2,1)} copy(bf16[16,192]{1,0:T(8,128)(2,1)} %get-tuple-element.5) | data formatting | bytes 12288

commit v4 on v3

--- a/solution.py
+++ b/solution.py
@@ -363,13 +363,13 @@
     across(5, 2)
     around(4, 1)
     complete(3)
+    text_heads()
     attend(0, 256, 2, 3)
     around(6, 0)
     across(6, 1)
     across(6, 3)
     across(6, 2)
     attend(256, 512, 2, 3)
-    text_heads()
     around(4, 2)
     around(5, 1)
     around(5, 3)
@@ -381,8 +381,6 @@
     complete(4)
     complete(6)
     complete(5)
-    arrived(kvt.at[pl.ds(0, (NCTX - 1) * TROWS)], tk_recv)
-    merge_weights(2)
 
     def exchange(c, low=NCH - 1):
         half = RCOUNT[c]
@@ -454,8 +452,10 @@
                     out[c - 1, j, half, :] = sums.astype(BF16)
                     start(out.at[c - 1, j, ref], recv.at[c - 1, j, ref], r_send, r_recv.at[way, c - 1, p, j], device)
 
-    exchange(4, 4)
     attend(0, 528, 4, NCH - 2)
+    arrived(kvt.at[pl.ds(0, (NCTX - 1) * TROWS)], tk_recv)
+    merge_weights(2)
+    exchange(4)
     exchange(3)
     reduce(4)
     exchange(2)

time: 98.7 us -> 101 us (1.023)
  the two profiles are of different devices: /device:TPU:2 before, /device:TPU:16 now
where the time goes in v4:
time: 101 us
  Pallas kernels  97.4 us (96%)
  local copies, waits for them, and re-layouts  2.91 us (3%)
    pallas_call x1, Pallas kernels, on_device(): pl.pallas_call(kernel, out_shape=(jax.ShapeDtypeStruct((ROWS, D), BF16),...  97.4 us
    unnamed x2, local copies, waits for them, and re-layouts  2.91 us

profile of v4, /device:TPU:16, one launch (start us, length us, event | category | flops | bytes accessed | tf_op | source)
XLA Modules:
  0.0 100.9 jit_solution(3247497549345175034)
XLA Ops:
  0.6 97.4 %joint_attention.1 = (bf16[32,3072]{1,0:T(8,128)(2,1)}, bf16[16,192]{1,0:T(8,128)(2,1)}) custom-call(bf16[32,3072]{1,0:T(8,128)(2,1)} %img_in.1, bf16[16,3072]{1,0:T(8,128)(2,1)} %txt_in.1, f32[3,3072]{1,0:T(4,128)} %imod_in.1, f32[3,3072]{1,0:T(4,128)} %tmod_in.1, bf16[3072,384]{1,0:T(8,128)(2,1)} %wp_in.1, bf16[192,384]{1,0:T(8,128)(2,1)} %wt_in.1, ...), custom_call_target="tpu_custom_call" | custom-call | flops 7000000000 | bytes 8000000 | tf_op jit(solution)/shard_map/joint_attention/pallas_call | solution.py:488
  98.0 1.6 %copy.13 = bf16[32,3072]{1,0:T(8,128)(2,1)} copy(bf16[32,3072]{1,0:T(8,128)(2,1)} %get-tuple-element.4) | data formatting | bytes 393216
  99.7 1.3 %copy.14 = bf16[16,192]{1,0:T(8,128)(2,1)} copy(bf16[16,192]{1,0:T(8,128)(2,1)} %get-tuple-element.5) | data formatting | bytes 12288
